TPU v7x, 512 devices: a whole 4x8x8 slice. The times are simulated.
512 devices in a mesh: row: 16 (over z, core), col: 32 (over x, y).
Axes of the slice: x: 4, y: 8, z: 8, core: 2. Of those that a mesh axis runs over, the one named last changes fastest.
Arguments:
- front: float32 [12288, 12288], P('row', 'col'), as said below
- structure: int32 [3, 96], replicated, may hold values from 0 to 1, as said below
- factor_front: float32 [3, 12288, 512], P(None, 'row', 'col'), may hold values from -0.0546875 to 0.0546875
- factor_border: float32 [2, 512, 512], replicated, may hold values from -0.6 to 0.6
- pivot_inverse: float32 [3, 512, 512], P(None, 'row')
Outputs:
- inverse_front: float32 [3, 512, 12288], P(None, 'row', 'col')
- inverse_parent: float32 [2, 512, 512], P(None, 'row')
- inverse_diagonal: float32 [3, 512, 512], P(None, 'row')
Inputs may be any that keep to these rules, and one draw needn't show every extreme that they name: front is exactly symmetric. structure[k, b] = 1 where front block b (rows b * 128 to (b + 1) * 128 - 1) lies in supernode k's structure; every 1 in row k is also a 1 in row k - 1; blocks b < 24 are 1 in every row.
All inputs are finite; a program needn't handle non-finite values.
Results may differ from a plain program's by a relative error of at most 0.0001.
Values sent between devices are 32-bit elements; how exact they have to be, the bound alone decides.
A program may use at most 64 MiB of HBM per device.

v0:
```python
import jax
import jax.numpy as jnp
from jax import lax
from jax.sharding import Mesh
from jax.sharding import PartitionSpec as P

BLK = 128
ROW = ("row_0", "row_1")
HIGH = lax.Precision.HIGHEST


def broadcast_by_axis(x, axes, root):
    x = jnp.where(lax.axis_index(axes) == root, x, jnp.zeros_like(x))
    for axis in axes:
        x = lax.psum(x, axis)
    return x


def split_up(x, dim, length):
    dims = x.shape
    pieces = x.reshape(*dims[:dim], length, dims[dim] // length, *dims[dim + 1 :])
    return jnp.moveaxis(pieces, dim, 0)


def sent_and_summed(x, axis, dim):
    length = lax.axis_size(axis)
    pieces = lax.all_to_all(split_up(x, dim, length), axis, 0, 0, tiled=True)
    return jnp.sum(pieces, axis=0)


def padded_to(lines, length):
    spare = -lines.shape[0] % length
    if not spare:
        return lines
    return jnp.concatenate([lines, jnp.zeros((spare, *lines.shape[1:]), lines.dtype)])


def in_order(pieces, dim):
    pieces = jnp.moveaxis(pieces, 0, dim)
    dims = pieces.shape
    return pieces.reshape(*dims[:dim], dims[dim] * dims[dim + 1], *dims[dim + 2 :])


def from_everyone(x, axis):
    copies = jnp.broadcast_to(x, (lax.axis_size(axis), *x.shape))
    return lax.all_to_all(copies, axis, split_axis=0, concat_axis=0, tiled=True)


def collect(x, axis, dim):
    return in_order(from_everyone(x, axis), dim)


def total_of(x, axes):
    lines = x.reshape(-1, x.shape[-1])
    own = sent_and_summed(padded_to(lines, lax.axis_size(axes)), axes, 0)
    whole = collect(own, axes, 0)
    return whole[: len(lines)].reshape(x.shape)


def matmul(former, latter):
    return jnp.dot(former, latter, precision=HIGH, preferred_element_type=jnp.float32)


def contract_first(former, latter):
    return lax.dot_general(
        former, latter, (((0,), (0,)), ((), ())), precision=HIGH, preferred_element_type=jnp.float32
    )


def block_flags(structure_row, first_row, rows_count):
    position = first_row + jnp.arange(rows_count, dtype=jnp.int32)
    owners = position // BLK
    numbers = jnp.arange(structure_row.shape[0], dtype=jnp.int32)
    matches = (owners[:, None] == numbers[None, :]).astype(jnp.float32)
    return jnp.dot(matches, structure_row.astype(jnp.float32), precision=HIGH)


def body(front, structure, factor_front, factor_border, pivot_inverse):
    row_index = lax.axis_index(ROW)
    col_index = lax.axis_index("col")
    rows_here = front.shape[0]
    cols_here = front.shape[1]
    width_here = pivot_inverse.shape[1]
    supers = structure.shape[0]
    row_first = row_index * rows_here
    col_first = col_index * cols_here
    fetched = lax.all_gather(factor_front, "col", axis=2, tiled=True)
    fronts = []
    parents = []
    diagonals = []
    previous = None
    diag_prev = None
    for section in range(supers):
        gathered = fetched[section]
        row_flags = block_flags(structure[section], row_first, rows_here)
        factor_rows = gathered * row_flags[:, None]
        own_half = lax.dynamic_slice_in_dim(factor_rows, col_index % 2 * cols_here, cols_here, 0)
        factor_cols = broadcast_by_axis(own_half, ROW, col_index // 2)
        partial_value = contract_first(factor_rows, front)
        if section > 0:
            border = factor_border[section - 1]
            border_rows = lax.dynamic_slice_in_dim(border, row_index * width_here, width_here, 0)
            partial_value = partial_value + contract_first(border_rows, previous)
            parent_part = total_of(matmul(previous, factor_cols), "col")
            parent_rows = parent_part + matmul(diag_prev, border)
            parent_all = lax.all_gather(parent_rows, ROW, axis=0, tiled=True)
            parents.append(-parent_rows)
        image_rows = sent_and_summed(partial_value, ROW, 0)
        col_flags = block_flags(structure[section], col_first, cols_here)
        current = -(image_rows * col_flags[None, :])
        gram_rows = total_of(matmul(image_rows, factor_cols), "col")
        diag_now = pivot_inverse[section] + gram_rows
        if section > 0:
            parent_slice = lax.dynamic_slice_in_dim(
                parent_all, row_index * width_here, width_here, 1
            )
            diag_now = diag_now + contract_first(parent_slice, border)
        fronts.append(current)
        diagonals.append(diag_now)
        previous = current
        diag_prev = diag_now
    return (jnp.stack(fronts), jnp.stack(parents), jnp.stack(diagonals))


def solution(mesh):
    torus = Mesh(mesh.devices.reshape(8, 2, mesh.shape["col"]), ("row_0", "row_1", "col"))
    return jax.shard_map(
        body,
        mesh=torus,
        in_specs=(P(ROW, "col"), P(), P(None, ROW, "col"), P(), P(None, ROW, None)),
        out_specs=(P(None, ROW, "col"), P(None, ROW, None), P(None, ROW, None)),
        check_vma=False,
    )
```

profile of v0, /device:TPU:1, one launch (start us, length us, event | category | flops | bytes accessed | tf_op | source)
XLA Modules:
  0.0 465.4 jit_solution(13938320989205049159)
XLA Ops:
  8.0 1.1 convolution_reduce_fusion.2
  9.1 1.1 convolution_reduce_fusion.1
  10.2 1.1 convolution_reduce_fusion
  11.3 91.5 %all-gather.4.cloned.1.call-done = f32[3,768,512]{1,2,0:T(8,128)} async-done(((f32[3,768,16]{1,2,0:T(8,128)}), f32[3,768,512]{1,2,0:T(8,128)}) %all-gather.4.cloned.1.call-update) | async-done | bytes 4718608 | tf_op jit(solution)/shard_map/all_gather | solution.py:87
  102.8 2.8 fusion
  105.6 1.0 dynamic-slice_select_fusion.2
  106.6 1.4 dynamic-slice_select_fusion
  108.1 87.4 %all-reduce.5.cloned.1.call-done = (f32[384,512]{0,1:T(8,128)}, f32[384,512]{0,1:T(8,128)}, f32[384,512]{0,1:T(8,128)}) async-done(((f32[384,512]{0,1:T(8,128)}, f32[384,512]{0,1:T(8,128)}, f32[384,512]{0,1:T(8,128)}), (f32[384,512]{0,1:T(8,128)}, f32[384,512]{0,1:T(8,128)}, f32[384,512]{0,1:T(8,128)})) %all-reduce.5.cloned.1.call-update) | async-done | bytes 2359312 | tf_op jit(solution)/shard_map/psum | solution.py:15
  195.5 3.6 fusion.3
  199.1 8.3 %all-to-all-start = ((f32[16,32,384]{2,1,0:T(8,128)}), f32[16,32,384]{2,1,0:T(8,128)}, u32[]{:S(2)}, u32[]{:S(2)}) async-start(f32[16,32,384]{2,1,0:T(8,128)} %fusion.3), calls=%async_computation | async-start | bytes 1572864 | tf_op jit(solution)/shard_map/all_to_all | solution.py:27
  207.8 22.4 %all-to-all-done = f32[16,32,384]{2,1,0:T(8,128)} async-done(((f32[16,32,384]{2,1,0:T(8,128)}), f32[16,32,384]{2,1,0:T(8,128)}, u32[]{:S(2)}, u32[]{:S(2)}) %all-to-all-start) | async-done | bytes 786464 | tf_op jit(solution)/shard_map/all_to_all | solution.py:27
  230.2 1.2 reduce_sum.78
  231.4 8.4 %all-reduce.7.cloned.1.call-done = (f32[384,512]{0,1:T(8,128)}, f32[384,512]{0,1:T(8,128)}, f32[384,512]{0,1:T(8,128)}) async-done(((f32[384,512]{0,1:T(8,128)}, f32[384,512]{0,1:T(8,128)}, f32[384,512]{0,1:T(8,128)}), (f32[384,512]{0,1:T(8,128)}, f32[384,512]{0,1:T(8,128)}, f32[384,512]{0,1:T(8,128)})) %all-reduce.7.cloned.1.call-update) | async-done | bytes 2359312 | tf_op jit(solution)/shard_map/psum | solution.py:15
  239.8 2.0 convolution_bitcast_fusion.3
  241.8 0.7 copy.9
  242.5 8.3 %all-to-all-start.5 = ((f32[32,1,512]{2,1,0:T(1,128)}), f32[32,1,512]{2,1,0:T(1,128)S(1)}, u32[]{:S(2)}, u32[]{:S(2)}) async-start(f32[32,1,512]{2,1,0:T(1,128)} %copy.9), calls=%async_computation.5 | async-start | bytes 131072 | tf_op jit(solution)/shard_map/all_to_all | solution.py:27
  250.8 2.0 convolution_bitcast_fusion.4
  252.7 0.7 copy.8
  253.4 6.2 %all-to-all-done.5 = f32[32,1,512]{2,1,0:T(1,128)S(1)} async-done(((f32[32,1,512]{2,1,0:T(1,128)}), f32[32,1,512]{2,1,0:T(1,128)S(1)}, u32[]{:S(2)}, u32[]{:S(2)}) %all-to-all-start.5) | async-done | bytes 65568 | tf_op jit(solution)/shard_map/all_to_all | solution.py:27
  259.6 3.9 all-to-all-start.3
  263.5 1.5 fusion.64
  265.1 7.3 %all-to-all-done.3 = f32[32,1,512]{2,1,0:T(1,128)S(1)} async-done(((f32[32,1,512]{2,1,0:T(1,128)}), f32[32,1,512]{2,1,0:T(1,128)S(1)}, u32[]{:S(2)}, u32[]{:S(2)}) %all-to-all-start.3) | async-done | bytes 65568 | tf_op jit(solution)/shard_map/all_to_all | solution.py:27
  273.0 3.9 all-to-all-start.6
  276.9 2.6 fusion.21
  279.5 6.2 %all-to-all-done.6 = f32[32,1,512]{2,1,0:T(1,128)S(1)} async-done(((f32[32,1,512]{2,1,0:T(1,128)}), f32[32,1,512]{2,1,0:T(1,128)S(1)}, u32[]{:S(2)}, u32[]{:S(2)}) %all-to-all-start.6) | async-done | bytes 65568 | tf_op jit(solution)/shard_map/all_to_all | solution.py:46
  286.4 3.9 all-to-all-start.4
  290.3 5.1 %convolution_add_fusion.1 = f32[512,384]{1,0:T(8,128)} fusion(f32[512,384]{1,0:T(8,128)} %fusion.21, f32[768,512]{0,1:T(8,128)} %copy-done.3, f32[768,384]{1,0:T(8,128)S(1)} %copy-done), kind=kOutput, calls=%fused_computation.7 | convolution fusion | flops 1812135936 | bytes 4325376 | tf_op jit(solution)/shard_map/dot_general | solution.py:65
  295.4 3.7 all-to-all-done.4
  299.1 12.6 %all-to-all-start.1 = ((f32[16,32,384]{2,1,0:T(8,128)}), f32[16,32,384]{2,1,0:T(8,128)}, u32[]{:S(2)}, u32[]{:S(2)}) async-start(f32[16,32,384]{2,1,0:T(8,128)} %bitcast.123), calls=%async_computation.1 | async-start | bytes 1572864 | tf_op jit(solution)/shard_map/all_to_all | solution.py:27
  312.0 0.9 bitcast_add_fusion.2
  312.8 2.2 convolution_add_fusion.3
  315.4 19.6 %all-to-all-done.1 = f32[16,32,384]{2,1,0:T(8,128)} async-done(((f32[16,32,384]{2,1,0:T(8,128)}), f32[16,32,384]{2,1,0:T(8,128)}, u32[]{:S(2)}, u32[]{:S(2)}) %all-to-all-start.1) | async-done | bytes 786464 | tf_op jit(solution)/shard_map/all_to_all | solution.py:27
  335.0 1.2 reduce_sum.80
  336.2 2.0 convolution_bitcast_fusion.2
  338.2 0.7 copy.10
  338.9 4.1 all-to-all-start.7
  343.0 2.0 convolution_bitcast_fusion.1
  345.0 0.7 copy.11
  345.7 6.2 %all-to-all-done.7 = f32[32,1,512]{2,1,0:T(1,128)S(1)} async-done(((f32[32,1,512]{2,1,0:T(1,128)}), f32[32,1,512]{2,1,0:T(1,128)S(1)}, u32[]{:S(2)}, u32[]{:S(2)}) %all-to-all-start.7) | async-done | bytes 65568 | tf_op jit(solution)/shard_map/all_to_all | solution.py:27
  352.5 3.9 all-to-all-start.9
  356.4 0.9 reduce_sum.86
  357.3 8.5 %all-to-all-done.9 = f32[32,1,512]{2,1,0:T(1,128)S(1)} async-done(((f32[32,1,512]{2,1,0:T(1,128)}), f32[32,1,512]{2,1,0:T(1,128)S(1)}, u32[]{:S(2)}, u32[]{:S(2)}) %all-to-all-start.9) | async-done | bytes 65568 | tf_op jit(solution)/shard_map/all_to_all | solution.py:27
  366.4 3.9 all-to-all-start.8
  370.3 2.6 fusion.19
  372.9 0.9 reduce_sum.87
  373.8 5.4 %all-to-all-done.8 = f32[32,1,512]{2,1,0:T(1,128)S(1)} async-done(((f32[32,1,512]{2,1,0:T(1,128)}), f32[32,1,512]{2,1,0:T(1,128)S(1)}, u32[]{:S(2)}, u32[]{:S(2)}) %all-to-all-start.8) | async-done | bytes 65568 | tf_op jit(solution)/shard_map/all_to_all | solution.py:46
  379.9 4.6 all-to-all-start.10
  384.4 5.1 %convolution_add_fusion = f32[512,384]{1,0:T(8,128)} fusion(f32[512,384]{1,0:T(8,128)} %fusion.19, f32[768,512]{0,1:T(8,128)} %copy-done.2, f32[768,384]{1,0:T(8,128)S(1)} %copy-done), kind=kOutput, calls=%fused_computation.6 | convolution fusion | flops 1812135936 | bytes 4325376 | tf_op jit(solution)/shard_map/dot_general | solution.py:65
  389.6 3.8 all-to-all-done.10
  393.4 7.4 %all-to-all-start.2 = ((f32[16,32,384]{2,1,0:T(8,128)}), f32[16,32,384]{2,1,0:T(8,128)}, u32[]{:S(2)}, u32[]{:S(2)}) async-start(f32[16,32,384]{2,1,0:T(8,128)} %bitcast.122), calls=%async_computation.2 | async-start | bytes 1572864 | tf_op jit(solution)/shard_map/all_to_all | solution.py:27
  400.9 1.7 convolution_add_fusion.5
  403.2 1.3 convolution_add_fusion.2
  404.6 0.9 convolution_reduce_fusion.3
  406.8 17.4 %all-to-all-done.2 = f32[16,32,384]{2,1,0:T(8,128)} async-done(((f32[16,32,384]{2,1,0:T(8,128)}), f32[16,32,384]{2,1,0:T(8,128)}, u32[]{:S(2)}, u32[]{:S(2)}) %all-to-all-start.2) | async-done | bytes 786464 | tf_op jit(solution)/shard_map/all_to_all | solution.py:27
  424.1 1.2 reduce_sum.82
  425.3 2.0 convolution_bitcast_fusion
  428.0 4.6 all-to-all-start.11
  432.6 1.5 pad_maximum_fusion.1
  434.1 7.3 %all-to-all-done.11 = f32[32,1,512]{2,1,0:T(1,128)} async-done(((f32[32,1,512]{2,1,0:T(1,128)}), f32[32,1,512]{2,1,0:T(1,128)}, u32[]{:S(2)}, u32[]{:S(2)}) %all-to-all-start.11) | async-done | bytes 65568 | tf_op jit(solution)/shard_map/all_to_all | solution.py:27
  441.4 0.9 reduce_sum.88
  442.9 4.5 all-to-all-start.12
  447.5 0.8 negate_bitcast_fusion
  449.0 7.4 %all-to-all-done.12 = f32[32,1,512]{2,1,0:T(1,128)} async-done(((f32[32,1,512]{2,1,0:T(1,128)}), f32[32,1,512]{2,1,0:T(1,128)}, u32[]{:S(2)}, u32[]{:S(2)}) %all-to-all-start.12) | async-done | bytes 65568 | tf_op jit(solution)/shard_map/all_to_all | solution.py:46
  456.4 1.7 fusion.5
  (54 shorter events, 9.9 us)
Async XLA Ops:
  7.2 188.4 %copy-start = (f32[768,384]{1,0:T(8,128)S(1)}, f32[768,384]{1,0:T(8,128)}, u32[]{:S(2)}) copy-start(f32[768,384]{1,0:T(8,128)} %param.5) | copy-start | bytes 3538948
  7.2 95.6 %all-gather.4.cloned.1.call-start = ((), (), s32[]{:S(2)}) async-start(), calls=%async_computation.13 | async-start | bytes 4866048 | tf_op jit(solution)/shard_map/all_gather | solution.py:87
  7.9 187.6 %all-reduce.5.cloned.1.call-start = ((), (), s32[]{:S(2)}) async-start(), calls=%async_computation.16 | async-start | bytes 4718592 | tf_op jit(solution)/shard_map/psum | solution.py:15
  105.6 2.4 copy-start.2
  105.6 2.4 copy-start.3
  108.0 131.8 %all-reduce.7.cloned.1.call-start = ((), (), s32[]{:S(2)}) async-start(), calls=%async_computation.17 | async-start | bytes 4718592 | tf_op jit(solution)/shard_map/psum | solution.py:15
  199.1 8.3 %copy-start.11 = (s32[3,96]{1,0:T(4,128)S(1)}, s32[3,96]{1,0:T(4,128)}, u32[]{:S(2)}) copy-start(s32[3,96]{1,0:T(4,128)} %param.6) | copy-start | bytes 3460
  199.1 31.1 %all-to-all-start = ((f32[16,32,384]{2,1,0:T(8,128)}), f32[16,32,384]{2,1,0:T(8,128)}, u32[]{:S(2)}, u32[]{:S(2)}) async-start(f32[16,32,384]{2,1,0:T(8,128)} %fusion.3), calls=%async_computation | async-start | bytes 1572864 | tf_op jit(solution)/shard_map/all_to_all | solution.py:27
  207.8 55.7 %copy-start.1 = (f32[2,512,512]{2,1,0:T(8,128)S(1)}, f32[2,512,512]{2,1,0:T(8,128)}, u32[]{:S(2)}) copy-start(f32[2,512,512]{2,1,0:T(8,128)} %param.8) | copy-start | bytes 6291460
  242.5 17.1 %all-to-all-start.5 = ((f32[32,1,512]{2,1,0:T(1,128)}), f32[32,1,512]{2,1,0:T(1,128)S(1)}, u32[]{:S(2)}, u32[]{:S(2)}) async-start(f32[32,1,512]{2,1,0:T(1,128)} %copy.9), calls=%async_computation.5 | async-start | bytes 131072 | tf_op jit(solution)/shard_map/all_to_all | solution.py:27
  259.6 12.7 %all-to-all-start.3 = ((f32[32,1,512]{2,1,0:T(1,128)}), f32[32,1,512]{2,1,0:T(1,128)S(1)}, u32[]{:S(2)}, u32[]{:S(2)}) async-start(f32[32,1,512]{2,1,0:T(1,128)} %copy.8), calls=%async_computation.3 | async-start | bytes 131072 | tf_op jit(solution)/shard_map/all_to_all | solution.py:27
  273.0 12.7 %all-to-all-start.6 = ((f32[32,1,512]{2,1,0:T(1,128)}), f32[32,1,512]{2,1,0:T(1,128)S(1)}, u32[]{:S(2)}, u32[]{:S(2)}) async-start(f32[32,1,512]{2,1,0:T(1,128)} %broadcast_in_dim.11), calls=%async_computation.6 | async-start | bytes 131072 | tf_op jit(solution)/shard_map/all_to_all | solution.py:46
  286.4 12.7 %all-to-all-start.4 = ((f32[32,1,512]{2,1,0:T(1,128)}), f32[32,1,512]{2,1,0:T(1,128)S(1)}, u32[]{:S(2)}, u32[]{:S(2)}) async-start(f32[32,1,512]{2,1,0:T(1,128)} %broadcast_in_dim.10), calls=%async_computation.4 | async-start | bytes 131072 | tf_op jit(solution)/shard_map/all_to_all | solution.py:46
  299.1 12.6 %copy-start.7 = (f32[32,1,512]{2,1,0:T(1,128)}, f32[32,1,512]{2,1,0:T(1,128)S(1)}, u32[]{:S(2)}) copy-start(f32[32,1,512]{2,1,0:T(1,128)S(1)} %all-to-all-done.4) | copy-start | bytes 196612
  299.1 35.9 %all-to-all-start.1 = ((f32[16,32,384]{2,1,0:T(8,128)}), f32[16,32,384]{2,1,0:T(8,128)}, u32[]{:S(2)}, u32[]{:S(2)}) async-start(f32[16,32,384]{2,1,0:T(8,128)} %bitcast.123), calls=%async_computation.1 | async-start | bytes 1572864 | tf_op jit(solution)/shard_map/all_to_all | solution.py:27
  311.7 89.1 %all-gather.6.cloned.1.call-start = ((), (), s32[]{:S(2)}) async-start(), calls=%async_computation.14 | async-start | bytes 1114112 | tf_op jit(solution)/shard_map/all_gather | solution.py:106
  338.9 13.0 %all-to-all-start.7 = ((f32[32,1,512]{2,1,0:T(1,128)}), f32[32,1,512]{2,1,0:T(1,128)S(1)}, u32[]{:S(2)}, u32[]{:S(2)}) async-start(f32[32,1,512]{2,1,0:T(1,128)} %copy.10), calls=%async_computation.7 | async-start | bytes 131072 | tf_op jit(solution)/shard_map/all_to_all | solution.py:27
  351.9 0.6 copy-start.9
  352.5 13.3 %all-to-all-start.9 = ((f32[32,1,512]{2,1,0:T(1,128)}), f32[32,1,512]{2,1,0:T(1,128)S(1)}, u32[]{:S(2)}, u32[]{:S(2)}) async-start(f32[32,1,512]{2,1,0:T(1,128)} %copy.11), calls=%async_computation.9 | async-start | bytes 131072 | tf_op jit(solution)/shard_map/all_to_all | solution.py:27
  365.8 0.7 copy-start.8
  366.4 12.7 %all-to-all-start.8 = ((f32[32,1,512]{2,1,0:T(1,128)}), f32[32,1,512]{2,1,0:T(1,128)S(1)}, u32[]{:S(2)}, u32[]{:S(2)}) async-start(f32[32,1,512]{2,1,0:T(1,128)} %broadcast_in_dim.12), calls=%async_computation.8 | async-start | bytes 131072 | tf_op jit(solution)/shard_map/all_to_all | solution.py:46
  379.9 13.5 %all-to-all-start.10 = ((f32[32,1,512]{2,1,0:T(1,128)}), f32[32,1,512]{2,1,0:T(1,128)}, u32[]{:S(2)}, u32[]{:S(2)}) async-start(f32[32,1,512]{2,1,0:T(1,128)} %broadcast_in_dim.13), calls=%async_computation.10 | async-start | bytes 131072 | tf_op jit(solution)/shard_map/all_to_all | solution.py:46
  393.4 30.7 %all-to-all-start.2 = ((f32[16,32,384]{2,1,0:T(8,128)}), f32[16,32,384]{2,1,0:T(8,128)}, u32[]{:S(2)}, u32[]{:S(2)}) async-start(f32[16,32,384]{2,1,0:T(8,128)} %bitcast.122), calls=%async_computation.2 | async-start | bytes 1572864 | tf_op jit(solution)/shard_map/all_to_all | solution.py:27
  400.8 55.6 %all-gather.8.cloned.1.call-start = ((), (), s32[]{:S(2)}) async-start(), calls=%async_computation.15 | async-start | bytes 1114112 | tf_op jit(solution)/shard_map/all_gather | solution.py:106
  402.6 0.6 copy-start.5
  404.6 42.9 %copy-start.4 = (f32[32,512]{1,0:T(8,128)S(1)}, f32[32,512]{1,0:T(8,128)}, u32[]{:S(2)}) copy-start(f32[32,512]{1,0:T(8,128)} %convolution_add_fusion.3) | copy-start | bytes 196612
  406.7 25.8 %copy-start.10 = (f32[384]{0:T(512)S(1)}, f32[384]{0:T(512)}, u32[]{:S(2)}) copy-start(f32[384]{0:T(512)} %convolution_reduce_fusion.3) | copy-start | bytes 4612
  427.3 30.9 %copy-start.6 = (f32[32,512]{1,0:T(8,128)S(1)}, f32[32,512]{1,0:T(8,128)}, u32[]{:S(2)}) copy-start(f32[32,512]{1,0:T(8,128)} %copy-done.5) | copy-start | bytes 196612
  428.0 13.4 %all-to-all-start.11 = ((f32[32,1,512]{2,1,0:T(1,128)}), f32[32,1,512]{2,1,0:T(1,128)}, u32[]{:S(2)}, u32[]{:S(2)}) async-start(f32[32,1,512]{2,1,0:T(1,128)} %copy.12), calls=%async_computation.11 | async-start | bytes 131072 | tf_op jit(solution)/shard_map/all_to_all | solution.py:27
  442.9 13.5 %all-to-all-start.12 = ((f32[32,1,512]{2,1,0:T(1,128)}), f32[32,1,512]{2,1,0:T(1,128)}, u32[]{:S(2)}, u32[]{:S(2)}) async-start(f32[32,1,512]{2,1,0:T(1,128)} %broadcast_in_dim.14), calls=%async_computation.12 | async-start | bytes 131072 | tf_op jit(solution)/shard_map/all_to_all | solution.py:46
Sparse Core Ops, SparseCore 0:
  11.2 91.5 all-gather.3
  108.1 87.3 all-reduce.4
  198.6 41.2 all-reduce.6
  315.2 39.2 all-gather.5
  404.7 38.7 all-gather.7
where the time goes:
time: 467 us; the launch traced here: 465 us
  waiting for transfers between devices  310 us (66%)
  starting transfers between devices  74.1 us (16%)
  matrix products  40.5 us (9%)
  other arithmetic  17.4 us (4%)
  between operations  14.1 us (3%)
  local copies, waits for them, and re-layouts  9.62 us (2%)
    psum x2, waiting for transfers between devices, broadcast_by_axis(): x = lax.psum(x, axis)  95.9 us
    all_to_all x8, waiting for transfers between devices, sent_and_summed(): pieces = lax.all_to_all(split_up(x, dim, length), axis, 0, 0, tiled=True)  94.9 us
    all_gather x1, waiting for transfers between devices, body(): fetched = lax.all_gather(factor_front, 'col', axis=2, tiled=True)  91.5 us
    all_to_all x8, starting transfers between devices, sent_and_summed(): pieces = lax.all_to_all(split_up(x, dim, length), axis, 0, 0, tiled=True)  53 us
    all_to_all x5, waiting for transfers between devices, from_everyone(): return lax.all_to_all(copies, axis, split_axis=0, concat_axis=0, tiled=True)  26.6 us
    dot_general x7, matrix products, contract_first(): lax.dot_general(former, latter, (((0,), (0,)), ((), ())), precision=HIGH,...  22.4 us
    all_to_all x5, starting transfers between devices, from_everyone(): return lax.all_to_all(copies, axis, split_axis=0, concat_axis=0, tiled=True)  20.7 us
    dot_general x7, matrix products, matmul(): jnp.dot(former, latter, precision=HIGH, preferred_element_type=jnp.float32)  13.3 us
  transfers between devices with their start and end apart: 18, of which 16 were waited for; matrix products, arithmetic and copies ran while one was open for 12% of the time, Pallas kernels for 0%

commit v1 on v0

--- a/solution.py
+++ b/solution.py
@@ -12,7 +12,8 @@
 def broadcast_by_axis(x, axes, root):
     x = jnp.where(lax.axis_index(axes) == root, x, jnp.zeros_like(x))
     for axis in axes:
-        x = lax.psum(x, axis)
+        found_now = jax.lax.all_gather(x, axis)
+        x = jnp.sum(found_now, axis=0)
     return x
 
 

time: 467 us -> 635 us (1.36); the launches traced: 465 us -> 625 us
  waiting for transfers between devices: 310 us -> 420 us
  other arithmetic: 17.4 us -> 38.5 us
  local copies, waits for them, and re-layouts: 9.62 us -> 30.6 us
  starting transfers between devices: 74.1 us -> 81 us
    all_gather x0 -> x6, waiting for transfers between devices: none -> 243 us  [broadcast_by_axis(): found_now = jax.lax.all_gather(x, axis)]
    psum x2 -> x0, waiting for transfers between devices: 95.9 us -> none  [broadcast_by_axis(): x = lax.psum(x, axis)]
    all_to_all x8, waiting for transfers between devices: 94.9 us -> 59.6 us  [sent_and_summed(): pieces = lax.all_to_all(split_up(x, dim, length), axis, 0, 0, tiled=True)]
    reduce_sum x0 -> x6, other arithmetic: none -> 18.8 us  [broadcast_by_axis(): x = jnp.sum(found_now, axis=0)]
    unnamed x24 -> x27, local copies, waits for them, and re-layouts: 1.3 us -> 14.3 us
    all_gather x0 -> x3, local copies, waits for them, and re-layouts: none -> 8.03 us  [broadcast_by_axis(): found_now = jax.lax.all_gather(x, axis)]
  transfers between devices with their start and end apart: 18 -> 22, of which waited for: 16 -> 16; matrix products, arithmetic and copies ran while one was open for 12% -> 16% of each run, Pallas kernels for 0% -> 0%
where the time goes in v1:
time: 635 us; the launch traced here: 625 us
  waiting for transfers between devices  420 us (66%)
  starting transfers between devices  81 us (13%)
  matrix products  40.2 us (6%)
  other arithmetic  38.5 us (6%)
  local copies, waits for them, and re-layouts  30.6 us (5%)
  between operations  14.5 us (2%)
    all_gather x6, waiting for transfers between devices, broadcast_by_axis(): found_now = jax.lax.all_gather(x, axis)  243 us
    all_gather x1, waiting for transfers between devices, body(): fetched = lax.all_gather(factor_front, 'col', axis=2, tiled=True)  91.5 us
    all_to_all x8, waiting for transfers between devices, sent_and_summed(): pieces = lax.all_to_all(split_up(x, dim, length), axis, 0, 0, tiled=True)  59.6 us
    all_to_all x8, starting transfers between devices, sent_and_summed(): pieces = lax.all_to_all(split_up(x, dim, length), axis, 0, 0, tiled=True)  59.1 us
    all_to_all x5, waiting for transfers between devices, from_everyone(): return lax.all_to_all(copies, axis, split_axis=0, concat_axis=0, tiled=True)  25.4 us
    dot_general x7, matrix products, contract_first(): lax.dot_general(former, latter, (((0,), (0,)), ((), ())), precision=HIGH,...  22.4 us
    all_to_all x5, starting transfers between devices, from_everyone(): return lax.all_to_all(copies, axis, split_axis=0, concat_axis=0, tiled=True)  21.1 us
    reduce_sum x6, other arithmetic, broadcast_by_axis(): x = jnp.sum(found_now, axis=0)  18.8 us
  transfers between devices with their start and end apart: 22, of which 16 were waited for; matrix products, arithmetic and copies ran while one was open for 16% of the time, Pallas kernels for 0%

profile of v1, /device:TPU:1, one launch (start us, length us, event | category | flops | bytes accessed | tf_op | source)
XLA Modules:
  0.0 625.2 jit_solution(4041857294623762418)
XLA Ops:
  8.0 1.1 convolution_reduce_fusion.2
  9.1 1.1 convolution_reduce_fusion.1
  11.3 91.5 %all-gather.16.cloned.1.call-done = f32[3,768,512]{1,2,0:T(8,128)} async-done(((f32[3,768,16]{1,2,0:T(8,128)}), f32[3,768,512]{1,2,0:T(8,128)}) %all-gather.16.cloned.1.call-update) | async-done | bytes 4718608 | tf_op jit(solution)/shard_map/all_gather | solution.py:88
  102.8 4.0 fusion
  106.7 1.1 copy-done.2
  109.9 2.1 dynamic-slice_select_fusion
  112.1 75.1 %all-gather.22.cloned.1.call-done = f32[3072,512]{0,1:T(8,128)} async-done(((f32[384,512]{0,1:T(8,128)}), f32[3072,512]{0,1:T(8,128)}) %all-gather.22.cloned.1.call-update) | async-done | bytes 6291472 | tf_op jit(solution)/shard_map/all_gather | solution.py:15
  187.2 4.2 copy.23
  191.4 2.8 bitcast_reduce_fusion.2
  194.2 3.5 fusion.3
  197.7 4.9 all-to-all-start
  202.6 79.5 %all-gather.26.cloned.1.call-done = f32[3072,512]{0,1:T(8,128)} async-done(((f32[384,512]{0,1:T(8,128)}), f32[3072,512]{0,1:T(8,128)}) %all-gather.26.cloned.1.call-update) | async-done | bytes 6291472 | tf_op jit(solution)/shard_map/all_gather | solution.py:15
  282.2 4.2 copy.24
  286.3 2.8 bitcast_reduce_fusion.1
  290.7 69.4 %all-gather.30.cloned.1.call-done = f32[3072,512]{0,1:T(8,128)} async-done(((f32[384,512]{0,1:T(8,128)}), f32[3072,512]{0,1:T(8,128)}) %all-gather.30.cloned.1.call-update) | async-done | bytes 6291472 | tf_op jit(solution)/shard_map/all_gather | solution.py:15
  360.1 4.2 copy.25
  364.3 2.8 bitcast_reduce_fusion
  367.1 12.5 %all-gather.24.cloned.1.call-done = f32[768,512]{0,1:T(8,128)} async-done(((f32[384,512]{0,1:T(8,128)}), f32[768,512]{0,1:T(8,128)}) %all-gather.24.cloned.1.call-update) | async-done | bytes 1572880 | tf_op jit(solution)/shard_map/all_gather | solution.py:15
  379.6 2.1 reshape.217
  381.7 1.9 reduce_sum.139
  383.6 1.7 convolution_bitcast_fusion.4
  386.0 8.3 %all-to-all-start.3 = ((f32[32,1,512]{2,1,0:T(1,128)}), f32[32,1,512]{2,1,0:T(1,128)S(1)}, u32[]{:S(2)}, u32[]{:S(2)}) async-start(f32[32,1,512]{2,1,0:T(1,128)} %copy.13), calls=%async_computation.3 | async-start | bytes 131072 | tf_op jit(solution)/shard_map/all_to_all | solution.py:28
  394.3 6.6 %all-gather.28.cloned.1.call-done = f32[768,512]{0,1:T(8,128)} async-done(((f32[384,512]{0,1:T(8,128)}), f32[768,512]{0,1:T(8,128)}) %all-gather.28.cloned.1.call-update) | async-done | bytes 1572880 | tf_op jit(solution)/shard_map/all_gather | solution.py:15
  400.8 2.9 reshape.219
  403.8 4.3 reduce_sum.142
  408.1 2.0 convolution_bitcast_fusion.3
  410.7 8.3 %all-to-all-start.5 = ((f32[32,1,512]{2,1,0:T(1,128)}), f32[32,1,512]{2,1,0:T(1,128)S(1)}, u32[]{:S(2)}, u32[]{:S(2)}) async-start(f32[32,1,512]{2,1,0:T(1,128)} %copy.14), calls=%async_computation.5 | async-start | bytes 131072 | tf_op jit(solution)/shard_map/all_to_all | solution.py:28
  419.0 1.5 fusion.64
  420.6 7.3 %all-to-all-done.5 = f32[32,1,512]{2,1,0:T(1,128)S(1)} async-done(((f32[32,1,512]{2,1,0:T(1,128)}), f32[32,1,512]{2,1,0:T(1,128)S(1)}, u32[]{:S(2)}, u32[]{:S(2)}) %all-to-all-start.5) | async-done | bytes 65568 | tf_op jit(solution)/shard_map/all_to_all | solution.py:28
  428.5 4.0 all-to-all-start.4
  432.6 2.6 fusion.21
  436.1 5.4 all-to-all-done.4
  442.1 3.9 all-to-all-start.6
  446.0 5.1 convolution_add_fusion.1
  451.1 3.7 all-to-all-done.6
  454.8 11.4 %all-to-all-start.1 = ((f32[16,32,384]{2,1,0:T(8,128)}), f32[16,32,384]{2,1,0:T(8,128)}, u32[]{:S(2)}, u32[]{:S(2)}) async-start(f32[16,32,384]{2,1,0:T(8,128)} %bitcast.147), calls=%async_computation.1 | async-start | bytes 1572864 | tf_op jit(solution)/shard_map/all_to_all | solution.py:28
  467.2 1.3 convolution_add_fusion.3
  468.9 20.7 %all-to-all-done.1 = f32[16,32,384]{2,1,0:T(8,128)} async-done(((f32[16,32,384]{2,1,0:T(8,128)}), f32[16,32,384]{2,1,0:T(8,128)}, u32[]{:S(2)}, u32[]{:S(2)}) %all-to-all-start.1) | async-done | bytes 786464 | tf_op jit(solution)/shard_map/all_to_all | solution.py:28
  489.6 1.2 reduce_sum.134
  490.7 2.0 convolution_bitcast_fusion.1
  493.4 4.1 all-to-all-start.9
  497.6 3.0 reshape.221
  500.5 4.2 reduce_sum.145
  504.7 2.0 convolution_bitcast_fusion.2
  507.4 9.4 %all-to-all-start.7 = ((f32[32,1,512]{2,1,0:T(1,128)}), f32[32,1,512]{2,1,0:T(1,128)}, u32[]{:S(2)}, u32[]{:S(2)}) async-start(f32[32,1,512]{2,1,0:T(1,128)} %copy.15), calls=%async_computation.7 | async-start | bytes 131072 | tf_op jit(solution)/shard_map/all_to_all | solution.py:28
  516.8 8.9 %all-to-all-done.7 = f32[32,1,512]{2,1,0:T(1,128)} async-done(((f32[32,1,512]{2,1,0:T(1,128)}), f32[32,1,512]{2,1,0:T(1,128)}, u32[]{:S(2)}, u32[]{:S(2)}) %all-to-all-start.7) | async-done | bytes 65568 | tf_op jit(solution)/shard_map/all_to_all | solution.py:28
  526.4 3.9 all-to-all-start.10
  530.2 2.6 fusion.19
  533.7 5.4 all-to-all-done.10
  539.8 4.8 all-to-all-start.8
  544.6 5.2 convolution_add_fusion
  549.7 3.7 all-to-all-done.8
  553.4 7.4 %all-to-all-start.2 = ((f32[16,32,384]{2,1,0:T(8,128)}), f32[16,32,384]{2,1,0:T(8,128)}, u32[]{:S(2)}, u32[]{:S(2)}) async-start(f32[16,32,384]{2,1,0:T(8,128)} %bitcast.146), calls=%async_computation.2 | async-start | bytes 1572864 | tf_op jit(solution)/shard_map/all_to_all | solution.py:28
  560.9 1.7 convolution_add_fusion.5
  563.2 2.2 convolution_add_fusion.2
  567.5 15.4 %all-to-all-done.2 = f32[16,32,384]{2,1,0:T(8,128)} async-done(((f32[16,32,384]{2,1,0:T(8,128)}), f32[16,32,384]{2,1,0:T(8,128)}, u32[]{:S(2)}, u32[]{:S(2)}) %all-to-all-start.2) | async-done | bytes 786464 | tf_op jit(solution)/shard_map/all_to_all | solution.py:28
  583.0 1.2 reduce_sum.136
  584.2 2.0 convolution_bitcast_fusion
  586.8 5.4 all-to-all-start.11
  592.2 1.5 pad_maximum_fusion.1
  593.7 7.3 %all-to-all-done.11 = f32[32,1,512]{2,1,0:T(1,128)} async-done(((f32[32,1,512]{2,1,0:T(1,128)}), f32[32,1,512]{2,1,0:T(1,128)}, u32[]{:S(2)}, u32[]{:S(2)}) %all-to-all-start.11) | async-done | bytes 65568 | tf_op jit(solution)/shard_map/all_to_all | solution.py:28
  602.6 4.6 all-to-all-start.12
  608.7 7.3 %all-to-all-done.12 = f32[32,1,512]{2,1,0:T(1,128)} async-done(((f32[32,1,512]{2,1,0:T(1,128)}), f32[32,1,512]{2,1,0:T(1,128)}, u32[]{:S(2)}, u32[]{:S(2)}) %all-to-all-start.12) | async-done | bytes 65568 | tf_op jit(solution)/shard_map/all_to_all | solution.py:47
  616.0 1.7 fusion.5
  (79 shorter events, 21.5 us)
Async XLA Ops:
  7.2 187.0 %copy-start = (f32[768,384]{1,0:T(8,128)S(1)}, f32[768,384]{1,0:T(8,128)}, u32[]{:S(2)}) copy-start(f32[768,384]{1,0:T(8,128)} %param.5) | copy-start | bytes 3538948
  7.2 95.6 %all-gather.16.cloned.1.call-start = ((), (), s32[]{:S(2)}) async-start(), calls=%async_computation.13 | async-start | bytes 4866048 | tf_op jit(solution)/shard_map/all_gather | solution.py:88
  7.9 179.3 %all-gather.22.cloned.1.call-start = ((), (), s32[]{:S(2)}) async-start(), calls=%async_computation.16 | async-start | bytes 7077888 | tf_op jit(solution)/shard_map/all_gather | solution.py:15
  106.7 1.1 copy-start.2
  108.8 173.3 %all-gather.26.cloned.1.call-start = ((), (), s32[]{:S(2)}) async-start(), calls=%async_computation.18 | async-start | bytes 7077888 | tf_op jit(solution)/shard_map/all_gather | solution.py:15
  109.9 250.2 %all-gather.30.cloned.1.call-start = ((), (), s32[]{:S(2)}) async-start(), calls=%async_computation.20 | async-start | bytes 7077888 | tf_op jit(solution)/shard_map/all_gather | solution.py:15
  112.0 267.5 %all-gather.24.cloned.1.call-start = ((), (), s32[]{:S(2)}) async-start(), calls=%async_computation.17 | async-start | bytes 2359296 | tf_op jit(solution)/shard_map/all_gather | solution.py:15
  197.7 92.3 %all-to-all-start = ((f32[16,32,384]{2,1,0:T(8,128)}), f32[16,32,384]{2,1,0:T(8,128)S(1)}, u32[]{:S(2)}, u32[]{:S(2)}) async-start(f32[16,32,384]{2,1,0:T(8,128)} %fusion.3), calls=%async_computation | async-start | bytes 1572864 | tf_op jit(solution)/shard_map/all_to_all | solution.py:28
  202.6 198.2 %all-gather.28.cloned.1.call-start = ((), (), s32[]{:S(2)}) async-start(), calls=%async_computation.19 | async-start | bytes 2359296 | tf_op jit(solution)/shard_map/all_gather | solution.py:15
  286.3 3.4 copy-start.11
  289.2 208.4 %all-gather.32.cloned.1.call-start = ((), (), s32[]{:S(2)}) async-start(), calls=%async_computation.21 | async-start | bytes 2359296 | tf_op jit(solution)/shard_map/all_gather | solution.py:15
  383.6 17.2 %copy-start.3 = (f32[384,512]{0,1:T(8,128)}, f32[384,512]{0,1:T(8,128)S(1)}, u32[]{:S(2)}) copy-start(f32[384,512]{0,1:T(8,128)S(1)} %reduce_sum.139) | copy-start | bytes 2359300
  386.0 24.7 %all-to-all-start.3 = ((f32[32,1,512]{2,1,0:T(1,128)}), f32[32,1,512]{2,1,0:T(1,128)S(1)}, u32[]{:S(2)}, u32[]{:S(2)}) async-start(f32[32,1,512]{2,1,0:T(1,128)} %copy.13), calls=%async_computation.3 | async-start | bytes 131072 | tf_op jit(solution)/shard_map/all_to_all | solution.py:28
  403.8 4.3 copy-start.4
  403.8 15.3 %copy-start.1 = (f32[2,512,512]{2,1,0:T(8,128)S(1)}, f32[2,512,512]{2,1,0:T(8,128)}, u32[]{:S(2)}) copy-start(f32[2,512,512]{2,1,0:T(8,128)} %param.8) | copy-start | bytes 6291460
  410.7 17.1 %all-to-all-start.5 = ((f32[32,1,512]{2,1,0:T(1,128)}), f32[32,1,512]{2,1,0:T(1,128)S(1)}, u32[]{:S(2)}, u32[]{:S(2)}) async-start(f32[32,1,512]{2,1,0:T(1,128)} %copy.14), calls=%async_computation.5 | async-start | bytes 131072 | tf_op jit(solution)/shard_map/all_to_all | solution.py:28
  427.9 0.7 copy-start.9
  428.5 12.9 %all-to-all-start.4 = ((f32[32,1,512]{2,1,0:T(1,128)}), f32[32,1,512]{2,1,0:T(1,128)S(1)}, u32[]{:S(2)}, u32[]{:S(2)}) async-start(f32[32,1,512]{2,1,0:T(1,128)} %broadcast_in_dim.10), calls=%async_computation.4 | async-start | bytes 131072 | tf_op jit(solution)/shard_map/all_to_all | solution.py:47
  442.1 12.7 %all-to-all-start.6 = ((f32[32,1,512]{2,1,0:T(1,128)}), f32[32,1,512]{2,1,0:T(1,128)S(1)}, u32[]{:S(2)}, u32[]{:S(2)}) async-start(f32[32,1,512]{2,1,0:T(1,128)} %broadcast_in_dim.11), calls=%async_computation.6 | async-start | bytes 131072 | tf_op jit(solution)/shard_map/all_to_all | solution.py:47
  454.8 11.4 %copy-start.8 = (f32[32,1,512]{2,1,0:T(1,128)}, f32[32,1,512]{2,1,0:T(1,128)S(1)}, u32[]{:S(2)}) copy-start(f32[32,1,512]{2,1,0:T(1,128)S(1)} %all-to-all-done.6) | copy-start | bytes 196612
  454.8 34.7 %all-to-all-start.1 = ((f32[16,32,384]{2,1,0:T(8,128)}), f32[16,32,384]{2,1,0:T(8,128)}, u32[]{:S(2)}, u32[]{:S(2)}) async-start(f32[16,32,384]{2,1,0:T(8,128)} %bitcast.147), calls=%async_computation.1 | async-start | bytes 1572864 | tf_op jit(solution)/shard_map/all_to_all | solution.py:28
  466.3 94.6 %all-gather.18.cloned.1.call-start = ((), (), s32[]{:S(2)}) async-start(), calls=%async_computation.14 | async-start | bytes 1114112 | tf_op jit(solution)/shard_map/all_gather | solution.py:107
  493.4 14.0 %all-to-all-start.9 = ((f32[32,1,512]{2,1,0:T(1,128)}), f32[32,1,512]{2,1,0:T(1,128)S(1)}, u32[]{:S(2)}, u32[]{:S(2)}) async-start(f32[32,1,512]{2,1,0:T(1,128)} %copy.16), calls=%async_computation.9 | async-start | bytes 131072 | tf_op jit(solution)/shard_map/all_to_all | solution.py:28
  507.4 18.3 %all-to-all-start.7 = ((f32[32,1,512]{2,1,0:T(1,128)}), f32[32,1,512]{2,1,0:T(1,128)}, u32[]{:S(2)}, u32[]{:S(2)}) async-start(f32[32,1,512]{2,1,0:T(1,128)} %copy.15), calls=%async_computation.7 | async-start | bytes 131072 | tf_op jit(solution)/shard_map/all_to_all | solution.py:28
  526.4 12.7 %all-to-all-start.10 = ((f32[32,1,512]{2,1,0:T(1,128)}), f32[32,1,512]{2,1,0:T(1,128)S(1)}, u32[]{:S(2)}, u32[]{:S(2)}) async-start(f32[32,1,512]{2,1,0:T(1,128)} %broadcast_in_dim.13), calls=%async_computation.10 | async-start | bytes 131072 | tf_op jit(solution)/shard_map/all_to_all | solution.py:47
  539.8 13.6 %all-to-all-start.8 = ((f32[32,1,512]{2,1,0:T(1,128)}), f32[32,1,512]{2,1,0:T(1,128)}, u32[]{:S(2)}, u32[]{:S(2)}) async-start(f32[32,1,512]{2,1,0:T(1,128)} %broadcast_in_dim.12), calls=%async_computation.8 | async-start | bytes 131072 | tf_op jit(solution)/shard_map/all_to_all | solution.py:47
  553.4 29.6 %all-to-all-start.2 = ((f32[16,32,384]{2,1,0:T(8,128)}), f32[16,32,384]{2,1,0:T(8,128)}, u32[]{:S(2)}, u32[]{:S(2)}) async-start(f32[16,32,384]{2,1,0:T(8,128)} %bitcast.146), calls=%async_computation.2 | async-start | bytes 1572864 | tf_op jit(solution)/shard_map/all_to_all | solution.py:28
  560.8 55.2 %all-gather.20.cloned.1.call-start = ((), (), s32[]{:S(2)}) async-start(), calls=%async_computation.15 | async-start | bytes 1114112 | tf_op jit(solution)/shard_map/all_gather | solution.py:107
  562.6 0.6 copy-start.6
  565.4 41.8 %copy-start.5 = (f32[32,512]{1,0:T(8,128)S(1)}, f32[32,512]{1,0:T(8,128)}, u32[]{:S(2)}) copy-start(f32[32,512]{1,0:T(8,128)} %convolution_add_fusion.3) | copy-start | bytes 196612
  567.5 24.7 %copy-start.10 = (f32[384]{0:T(512)S(1)}, f32[384]{0:T(512)}, u32[]{:S(2)}) copy-start(f32[384]{0:T(512)} %convolution_reduce_fusion.3) | copy-start | bytes 4612
  586.1 31.6 %copy-start.7 = (f32[32,512]{1,0:T(8,128)S(1)}, f32[32,512]{1,0:T(8,128)}, u32[]{:S(2)}) copy-start(f32[32,512]{1,0:T(8,128)} %copy-done.6) | copy-start | bytes 196612
  586.8 14.2 %all-to-all-start.11 = ((f32[32,1,512]{2,1,0:T(1,128)}), f32[32,1,512]{2,1,0:T(1,128)}, u32[]{:S(2)}, u32[]{:S(2)}) async-start(f32[32,1,512]{2,1,0:T(1,128)} %copy.17), calls=%async_computation.11 | async-start | bytes 131072 | tf_op jit(solution)/shard_map/all_to_all | solution.py:28
  602.6 13.4 %all-to-all-start.12 = ((f32[32,1,512]{2,1,0:T(1,128)}), f32[32,1,512]{2,1,0:T(1,128)}, u32[]{:S(2)}, u32[]{:S(2)}) async-start(f32[32,1,512]{2,1,0:T(1,128)} %broadcast_in_dim.14), calls=%async_computation.12 | async-start | bytes 131072 | tf_op jit(solution)/shard_map/all_to_all | solution.py:47
Sparse Core Ops, SparseCore 0:
  11.2 91.5 all-gather.15
  109.0 78.1 all-gather.21
  189.3 92.8 all-gather.25
  284.1 75.9 all-gather.29
  362.1 17.4 all-gather.23
  381.5 19.2 all-gather.27
  402.9 19.2 all-gather.31
  469.8 39.2 all-gather.17
  565.5 38.3 all-gather.19
